TPU v7x, 512 devices: a whole 4x8x8 slice. The times are simulated.
512 devices in a mesh: dp: 32 (over z, y_hi), segment: 2 (over y_lo), mp: 8 (over x, core).
Axes of the slice: x: 4, y: 8 (y_hi: 4, y_lo: 2; y = y_hi * 2 + y_lo), z: 8, core: 2. Of those that a mesh axis runs over, the one named last changes fastest.
Arguments:
- prefix_hidden: bfloat16 [64, 512, 8192], P(('dp', 'segment'), 'mp'), may hold values from -16 to 16
- norm_gain: float32 [8192], replicated, may hold values from 0.5 to 1.5
- kv_weight: bfloat16 [8192, 2, 1024], P('dp', None, 'mp'), may hold values from -0.0625 to 0.0625
- action_query: bfloat16 [64, 128, 2048], P(('dp', 'segment'), None, 'mp'), may hold values from -104 to 104
- action_kv: bfloat16 [64, 128, 2, 1024], P(('dp', 'segment'), None, None, 'mp'), may hold values from -4.25 to 4.25
- out_cotangent: bfloat16 [64, 128, 2048], P(('dp', 'segment'), None, 'mp'), may hold values from -18 to 18
- prefix_blocks: int32 [64, 512], P(('dp', 'segment')), may hold values from 0 to 7, as said below
- action_blocks: int32 [64, 128], P(('dp', 'segment')), may hold values from 0 to 8, as said below
- prefix_lengths: int32 [64], P(('dp', 'segment')), may hold values from 128 to 512, as said below
- timesteps: int32 [64], P(('dp', 'segment')), may hold values from 0 to 999
Outputs:
- attn_out: bfloat16 [64, 128, 2048], P(('dp', 'segment'), None, 'mp')
- query_grad: float32 [64, 128, 2048], P(('dp', 'segment'), None, 'mp')
- action_kv_grad: float32 [64, 128, 2, 1024], P(('dp', 'segment'), None, None, 'mp')
- weight_grad: float32 [8192, 2, 1024], P('dp', None, 'mp')
Inputs may be any that keep to these rules, and one draw needn't show every extreme that they name: `prefix_blocks`: constant over each run of 64 positions, 0 on the first run, rising by 0 or 1 from one run to the next; in every draw some sample rises at every run. `action_blocks`: constant over each run of 64 positions; the last run of every sample holds 8; in every draw some sample's first run holds 0. `prefix_lengths`: in every draw some sample's prefix is whole and some sample's is 128.
All inputs are finite; a program needn't handle non-finite values.
Results may differ from a plain program's by a relative error of at most 0.017.
Values may be sent and summed in bfloat16 or wider, within the bound.
No kernel may reach another device: no remote copies, remote signals or barrier semaphores. Data moves between devices by JAX's collectives and lax.ppermute only.
A program may use at most 64 MiB of HBM per device.

v0:
```python
import jax
import jax.numpy as jnp
from jax import lax
from jax.sharding import Mesh
from jax.sharding import PartitionSpec as P

KVH = 8
HD = 128
QH = 16
STEPS = 1000
DP = ("dp_0", "dp_1")
DP_SEGMENT = ("dp_0", "dp_1", "segment")
EPS = 1e-06
NEGATIVE = -1e30


def sum_by_axis(terms, axes):
    subtotal = terms.astype(jnp.bfloat16)
    for axis in axes:
        subtotal = lax.psum_scatter(subtotal, axis, scatter_dimension=0, tiled=True)
    return subtotal.astype(jnp.float32)


def from_everyone(array, axis):
    copies = jnp.broadcast_to(array, (lax.axis_size(axis), *array.shape))
    return lax.all_to_all(copies, axis, split_axis=0, concat_axis=0, tiled=True)


def taken_together(array, axis):
    everything = from_everyone(array, axis)
    return jnp.sum(everything.astype(jnp.float32), axis=0)


def head_scores(query, keys):
    return jnp.einsum("agrh,jgh->graj", query, keys, preferred_element_type=jnp.float32) * HD ** (
        -0.5
    )


def backward_terms(probs, values, keys, query, grad_out):
    probs_low = probs.astype(jnp.bfloat16)
    d_probs = jnp.einsum("agrh,jgh->graj", grad_out, values, preferred_element_type=jnp.float32)
    delta = jnp.sum(probs * d_probs, axis=-1, keepdims=True)
    d_scores = (probs * (d_probs - delta)).astype(jnp.bfloat16)
    d_query = jnp.einsum(
        "graj,jgh->agrh", d_scores, keys, preferred_element_type=jnp.float32
    ) * HD ** (-0.5)
    d_keys = jnp.einsum(
        "graj,agrh->jgh", d_scores, query, preferred_element_type=jnp.float32
    ) * HD ** (-0.5)
    d_values = jnp.einsum("graj,agrh->jgh", probs_low, grad_out, preferred_element_type=jnp.float32)
    return (d_query, jnp.stack([d_keys, d_values], axis=1))


def shards(
    prefix_hidden,
    norm_gain,
    kv_weight,
    action_query,
    action_kv,
    out_cotangent,
    prefix_blocks,
    action_blocks,
    prefix_lengths,
    timesteps,
):
    acts = action_query.shape[1]
    heads_kv = kv_weight.shape[2] // HD
    ratio = QH // KVH
    columns = 2 * kv_weight.shape[2]
    wide = prefix_hidden[0].astype(jnp.float32)
    inverse = lax.rsqrt(jnp.mean(wide * wide, axis=-1, keepdims=True) + EPS)
    normed_local = (wide * inverse * norm_gain).astype(jnp.bfloat16)
    normed = lax.all_gather(normed_local, "mp", axis=0, tiled=True)
    rows = normed.shape[0]
    piece = lax.all_gather(kv_weight, DP, axis=0, tiled=True)
    section = normed
    projected = jnp.dot(
        section, piece.reshape(piece.shape[0], columns), preferred_element_type=jnp.float32
    )
    prefix_kv = projected.astype(jnp.bfloat16).reshape(rows, 2, heads_kv, HD)
    own_pair = action_kv[0].reshape(acts, 2, heads_kv, HD)
    query = action_query[0].reshape(acts, heads_kv, ratio, HD)
    flow_weight = 0.5 + (timesteps[0].astype(jnp.float32) + 0.5) / STEPS
    grad_out = (
        (flow_weight * out_cotangent[0].astype(jnp.float32))
        .astype(jnp.bfloat16)
        .reshape(acts, heads_kv, ratio, HD)
    )
    pblocks = prefix_blocks[0]
    ablocks = action_blocks[0]
    length = prefix_lengths[0]
    keys = jnp.concatenate([prefix_kv[:, 0], own_pair[:, 0]], axis=0)
    values = jnp.concatenate([prefix_kv[:, 1], own_pair[:, 1]], axis=0)
    positions = jnp.arange(rows, dtype=jnp.int32)
    see_prefix = (pblocks[None, :] <= ablocks[:, None]) & (positions[None, :] < length)
    see_action = ablocks[None, :] <= ablocks[:, None]
    visible = jnp.concatenate([see_prefix, see_action], axis=1)
    masked = jnp.where(visible, head_scores(query, keys), NEGATIVE)
    top = jnp.max(masked, axis=-1, keepdims=True)
    expo = jnp.where(visible, jnp.exp(masked - top), 0.0)
    probs = expo / jnp.sum(expo, axis=-1, keepdims=True)
    out = jnp.einsum(
        "graj,jgh->agrh", probs.astype(jnp.bfloat16), values, preferred_element_type=jnp.float32
    )
    d_query, d_pair = backward_terms(probs, values, keys, query, grad_out)
    d_prefix = d_pair[:rows]
    d_action = d_pair[rows:]
    attn_out = out.astype(jnp.bfloat16).reshape(1, acts, ratio * heads_kv * HD)
    query_grad = d_query.reshape(1, acts, ratio * heads_kv * HD)
    action_kv_grad = d_action.reshape(1, acts, 2, heads_kv * HD)
    prefix_grad = d_prefix.astype(jnp.bfloat16).reshape(rows, columns)
    section = normed
    term = lax.dot_general(
        section, prefix_grad, (((0,), (0,)), ((), ())), preferred_element_type=jnp.float32
    )
    shard = sum_by_axis(term.reshape(kv_weight.shape[0] * lax.axis_size(DP), 2, columns // 2), DP)
    weight_grad = taken_together(shard.astype(jnp.bfloat16), "segment").astype(jnp.float32)
    return (attn_out, query_grad, action_kv_grad, weight_grad)


def solution(mesh):
    torus = Mesh(
        mesh.devices.reshape(8, 4, mesh.shape["segment"], mesh.shape["mp"]),
        ("dp_0", "dp_1", "segment", "mp"),
    )
    placed = (
        P(DP_SEGMENT, "mp", None),
        P(),
        P(DP, None, "mp"),
        P(DP_SEGMENT, None, "mp"),
        P(DP_SEGMENT, None, None, "mp"),
        P(DP_SEGMENT, None, "mp"),
        P(DP_SEGMENT, None),
        P(DP_SEGMENT, None),
        P(DP_SEGMENT),
        P(DP_SEGMENT),
    )
    return jax.shard_map(
        shards,
        mesh=torus,
        in_specs=placed,
        out_specs=(
            P(DP_SEGMENT, None, "mp"),
            P(DP_SEGMENT, None, "mp"),
            P(DP_SEGMENT, None, None, "mp"),
            P(DP, None, "mp"),
        ),
        check_vma=False,
    )
```

profile of v0, /device:TPU:18, one launch (start us, length us, event | category | flops | bytes accessed | tf_op | source)
XLA Modules:
  0.0 294.3 jit_solution(14425961718619464857)
XLA Ops:
  7.3 0.7 all-gather.5.cloned.1.call-update
  8.0 1.5 fusion.4
  9.5 2.6 fusion.6
  12.2 0.0 reduce-scatter.3.cloned.1.call-start
  12.2 0.1 copy.52
  12.4 0.1 copy.77
  13.8 0.1 copy.78
  14.0 0.1 broadcast_compare_fusion
  14.1 0.2 compare_and_fusion
  14.3 102.6 %all-gather.5.cloned.1.call-done = bf16[8192,2,128]{2,1,0:T(2,128)(2,1)} async-done(((bf16[256,2,128]{2,1,0:T(2,128)(2,1)}), bf16[8192,2,128]{2,1,0:T(2,128)(2,1)}) %all-gather.5.cloned.1.call-update) | async-done | bytes 4194320 | tf_op jit(solution)/shard_map/all_gather | solution.py:76
  116.9 54.1 %all-gather.3.cloned.1.call-done = bf16[512,8192]{1,0:T(8,128)(2,1)} async-done(((bf16[64,8192]{1,0:T(8,128)(2,1)}), bf16[512,8192]{1,0:T(8,128)(2,1)}) %all-gather.3.cloned.1.call-update) | async-done | bytes 8388624 | tf_op jit(solution)/shard_map/all_gather | solution.py:74
  170.9 6.9 %fusion.8 = bf16[512,256]{0,1:T(8,128)(2,1)S(1)} fusion(bf16[512,8192]{1,0:T(8,128)(2,1)} %all-gather.3.cloned.1.call-done, bf16[1024,8,2,128]{3,2,1,0:T(2,128)(2,1)} %bitcast.129), kind=kOutput, calls=%fused_computation.13 | convolution fusion | flops 2147614720 | bytes 12845056 | tf_op jit(solution)/shard_map/dot_general | solution.py:78
  177.9 0.1 copy.76
  178.0 0.3 fusion.33
  178.3 0.1 fusion.15
  178.5 0.3 convolution_bitcast_fusion.1
  178.8 0.3 multiply_reduce_fusion
  179.1 0.2 fusion.17
  179.3 0.2 fusion.13
  179.6 2.3 copy-done.5
  181.8 4.0 %convolution_convert_fusion = bf16[8192,2,128]{2,0,1:T(8,128)(2,1)} fusion(bf16[512,8192]{1,0:T(8,128)(2,1)S(1)} %copy-done.5, f32[640,1,1,128]{0,3,2,1:T(8,128)S(1)} %convolution_bitcast_fusion.1, f32[640,1,1,128]{0,3,2,1:T(8,128)S(1)} %fusion.13), kind=kOutput, calls=%fused_computation | convolution fusion | flops 2150105088 | bytes 13238272 | tf_op jit(solution)/shard_map/dot_general | solution.py:114
  185.9 59.9 %reduce-scatter.3.cloned.1.call-done = bf16[1024,2,128]{2,0,1:T(8,128)(2,1)} async-done(((bf16[8192,2,128]{2,0,1:T(8,128)(2,1)}), bf16[1024,2,128]{2,0,1:T(8,128)(2,1)}) %reduce-scatter.3.cloned.1.call-update) | async-done | bytes 524304 | tf_op jit(solution)/shard_map/reduce_scatter | solution.py:20
  245.8 0.3 convolution_convert_fusion.1
  246.1 0.7 copy.64
  246.8 29.7 %reduce-scatter.5.cloned.1.call-done = bf16[256,2,128]{2,0,1:T(8,128)(2,1)} async-done(((bf16[1024,2,128]{2,0,1:T(8,128)(2,1)}), bf16[256,2,128]{2,0,1:T(8,128)(2,1)}) %reduce-scatter.5.cloned.1.call-update) | async-done | bytes 131088 | tf_op jit(solution)/shard_map/reduce_scatter | solution.py:20
  276.6 1.6 broadcast_in_dim.24
  278.2 3.4 %all-to-all-start = ((bf16[2,256,2,128]{3,1,2,0:T(8,128)(2,1)}), bf16[2,256,2,128]{3,1,2,0:T(8,128)(2,1)S(1)}, u32[]{:S(2)}, u32[]{:S(2)}) async-start(bf16[2,256,2,128]{3,1,2,0:T(8,128)(2,1)} %broadcast_in_dim.24), calls=%async_computation.2 | async-start | bytes 524288 | tf_op jit(solution)/shard_map/all_to_all | solution.py:26
  281.7 0.3 convolution_multiply_fusion.1
  281.9 0.8 copy.65
  282.7 0.8 copy.66
  283.4 3.4 %all-to-all-done = bf16[2,256,2,128]{3,1,2,0:T(8,128)(2,1)S(1)} async-done(((bf16[2,256,2,128]{3,1,2,0:T(8,128)(2,1)}), bf16[2,256,2,128]{3,1,2,0:T(8,128)(2,1)S(1)}, u32[]{:S(2)}, u32[]{:S(2)}) %all-to-all-start) | async-done | bytes 262176 | tf_op jit(solution)/shard_map/all_to_all | solution.py:26
  286.8 0.9 copy.67
  (27 shorter events, 0.3 us)
Async XLA Ops:
  7.2 5.0 %copy-start = (bf16[1,128,2,128]{3,2,1,0:T(2,128)(2,1)S(1)}, bf16[1,128,2,128]{3,2,1,0:T(2,128)(2,1)}, u32[]{:S(2)}) copy-start(bf16[1,128,2,128]{3,2,1,0:T(2,128)(2,1)} %param.14) | copy-start | bytes 196612
  7.2 5.2 %copy-start.1 = (bf16[1,128,256]{2,1,0:T(8,128)(2,1)S(1)}, bf16[1,128,256]{2,1,0:T(8,128)(2,1)}, u32[]{:S(2)}) copy-start(bf16[1,128,256]{2,1,0:T(8,128)(2,1)} %param.13) | copy-start | bytes 196612
  7.2 6.6 %copy-start.2 = (bf16[1,128,256]{2,1,0:T(8,128)(2,1)S(1)}, bf16[1,128,256]{2,1,0:T(8,128)(2,1)}, u32[]{:S(2)}) copy-start(bf16[1,128,256]{2,1,0:T(8,128)(2,1)} %param.15) | copy-start | bytes 196612
  7.2 6.8 %copy-start.3 = (s32[1,128]{1,0:T(1,128)S(1)}, s32[1,128]{1,0:T(1,128)}, u32[]{:S(2)}) copy-start(s32[1,128]{1,0:T(1,128)} %param.17) | copy-start | bytes 1540
  7.2 6.9 %copy-start.4 = (s32[1,512]{1,0:T(1,128)S(1)}, s32[1,512]{1,0:T(1,128)}, u32[]{:S(2)}) copy-start(s32[1,512]{1,0:T(1,128)} %param.16) | copy-start | bytes 6148
  7.2 109.6 %all-gather.5.cloned.1.call-start = ((), (), s32[]{:S(2)}) async-start(), calls=%async_computation.4 | async-start | bytes 4325376 | tf_op jit(solution)/shard_map/all_gather | solution.py:76
  8.0 163.0 %all-gather.3.cloned.1.call-start = ((), (), s32[]{:S(2)}) async-start(), calls=%async_computation.3 | async-start | bytes 9437184 | tf_op jit(solution)/shard_map/all_gather | solution.py:74
  12.2 233.6 %reduce-scatter.3.cloned.1.call-start = ((), (), s32[]{:S(2)}) async-start(), calls=%async_computation.5 | async-start | bytes 4718592 | tf_op jit(solution)/shard_map/reduce_scatter | solution.py:20
  178.5 3.4 %copy-start.5 = (bf16[512,8192]{1,0:T(8,128)(2,1)S(1)}, bf16[512,8192]{1,0:T(8,128)(2,1)}, u32[]{:S(2)}) copy-start(bf16[512,8192]{1,0:T(8,128)(2,1)} %all-gather.3.cloned.1.call-done) | copy-start | bytes 25165828
  185.8 90.7 %reduce-scatter.5.cloned.1.call-start = ((), (), s32[]{:S(2)}) async-start(), calls=%async_computation.6 | async-start | bytes 655360 | tf_op jit(solution)/shard_map/reduce_scatter | solution.py:20
  278.2 8.6 %all-to-all-start = ((bf16[2,256,2,128]{3,1,2,0:T(8,128)(2,1)}), bf16[2,256,2,128]{3,1,2,0:T(8,128)(2,1)S(1)}, u32[]{:S(2)}, u32[]{:S(2)}) async-start(bf16[2,256,2,128]{3,1,2,0:T(8,128)(2,1)} %broadcast_in_dim.24), calls=%async_computation.2 | async-start | bytes 524288 | tf_op jit(solution)/shard_map/all_to_all | solution.py:26
Sparse Core Ops, SparseCore 0:
  11.2 105.6 all-gather.4
  119.0 51.8 all-gather.2
  185.9 59.7 reduce-scatter.2
  248.4 28.1 reduce-scatter.4
where the time goes:
time: 295 us; the launch traced here: 294 us
  waiting for transfers between devices  250 us (85%)
  between operations  15.3 us (5%)
  matrix products  12.6 us (4%)
  local copies, waits for them, and re-layouts  7.58 us (3%)
  other arithmetic  4.84 us (2%)
  starting transfers between devices  3.6 us (1%)
    all_gather x1, waiting for transfers between devices, shards(): piece = lax.all_gather(kv_weight, DP, axis=0, tiled=True)  103 us
    reduce_scatter x2, waiting for transfers between devices, sum_by_axis(): subtotal = lax.psum_scatter(subtotal, axis, scatter_dimension=0, tiled=True)  89.6 us
    all_gather x1, waiting for transfers between devices, shards(): normed = lax.all_gather(normed_local, 'mp', axis=0, tiled=True)  54.1 us
    dot_general x1, matrix products, shards(): jnp.dot(section, piece.reshape(piece.shape[0], columns), preferred_elemen...  6.94 us
  transfers between devices with their start and end apart: 5, of which 5 were waited for; matrix products, arithmetic and copies ran while one was open for 3% of the time, Pallas kernels for 0%

commit v1 on v0

--- a/solution.py
+++ b/solution.py
@@ -71,7 +71,16 @@
     wide = prefix_hidden[0].astype(jnp.float32)
     inverse = lax.rsqrt(jnp.mean(wide * wide, axis=-1, keepdims=True) + EPS)
     normed_local = (wide * inverse * norm_gain).astype(jnp.bfloat16)
-    normed = lax.all_gather(normed_local, "mp", axis=0, tiled=True)
+    ways = lax.axis_size("mp")
+    up = [(d, (d + 1) % ways) for d in range(ways)]
+    down = [(d, (d - 1) % ways) for d in range(ways)]
+    earlier, later = ([normed_local], [normed_local])
+    for _ in range(ways // 2):
+        earlier.append(lax.ppermute(earlier[-1], "mp", up))
+    for _ in range((ways - 1) // 2):
+        later.append(lax.ppermute(later[-1], "mp", down))
+    line = jnp.concatenate([*earlier[::-1], *later[1:]], axis=0)
+    normed = jnp.roll(line, (lax.axis_index("mp") - ways // 2) * normed_local.shape[0], axis=0)
     rows = normed.shape[0]
     piece = lax.all_gather(kv_weight, DP, axis=0, tiled=True)
     section = normed

time: 295 us -> 259 us (0.88)
  waiting for transfers between devices: 250 us -> 137 us
  local copies, waits for them, and re-layouts: 7.58 us -> 65.1 us
  matrix products: 12.6 us -> 22.3 us
  starting transfers between devices: 3.6 us -> 9.21 us
    all_gather x1, waiting for transfers between devices: 103 us -> 0.02 us  [shards(): piece = lax.all_gather(kv_weight, DP, axis=0, tiled=True)]
    all_gather x1 -> x0, waiting for transfers between devices: 54.1 us -> none  [shards(): normed = lax.all_gather(normed_local, 'mp', axis=0, tiled=True)]
    concatenate x0 -> x1, local copies, waits for them, and re-layouts: none -> 37.6 us  [shards(): jnp.roll(line, (lax.axis_index('mp') - ways // 2) * normed_local.shape[0]...]
    ppermute x0 -> x7, waiting for transfers between devices: none -> 36.2 us  [the longest x4 36.2 us: shards(): earlier.append(lax.ppermute(earlier[-1], 'mp', up))]
    ppermute x0 -> x7, local copies, waits for them, and re-layouts: none -> 18.2 us  [the longest x4 10 us: shards(): earlier.append(lax.ppermute(earlier[-1], 'mp', up))]
    reduce_scatter x2, waiting for transfers between devices: 89.6 us -> 97.6 us  [sum_by_axis(): subtotal = lax.psum_scatter(subtotal, axis, scatter_dimension=0, tiled=True)]
    dot_general x1, matrix products: 3.96 us -> 11.1 us  [shards(): lax.dot_general(section, prefix_grad, (((0,), (0,)), ((), ())), preferred...]
    ppermute x0 -> x7, starting transfers between devices: none -> 5.65 us  [the longest x3 5.64 us: shards(): later.append(lax.ppermute(later[-1], 'mp', down))]
  transfers between devices with their start and end apart: 5 -> 11, of which waited for: 5 -> 6; matrix products, arithmetic and copies ran while one was open for 3% -> 27% of each run, Pallas kernels for 0% -> 0%
where the time goes in v1:
time: 259 us; the launch traced here: 256 us
  waiting for transfers between devices  137 us (53%)
  local copies, waits for them, and re-layouts  65.1 us (25%)
  matrix products  22.3 us (9%)
  between operations  15.3 us (6%)
  starting transfers between devices  9.21 us (4%)
  other arithmetic  6.46 us (2%)
    reduce_scatter x2, waiting for transfers between devices, sum_by_axis(): subtotal = lax.psum_scatter(subtotal, axis, scatter_dimension=0, tiled=True)  97.6 us
    concatenate x1, local copies, waits for them, and re-layouts, shards(): jnp.roll(line, (lax.axis_index('mp') - ways // 2) * normed_local.shape[0]...  37.6 us
    ppermute x4, waiting for transfers between devices, shards(): earlier.append(lax.ppermute(earlier[-1], 'mp', up))  36.2 us
    dot_general x1, matrix products, shards(): lax.dot_general(section, prefix_grad, (((0,), (0,)), ((), ())), preferred...  11.1 us
    ppermute x4, local copies, waits for them, and re-layouts, shards(): earlier.append(lax.ppermute(earlier[-1], 'mp', up))  10 us
    dot_general x1, matrix products, shards(): jnp.dot(section, piece.reshape(piece.shape[0], columns), preferred_elemen...  9.54 us
    ppermute x3, local copies, waits for them, and re-layouts, shards(): later.append(lax.ppermute(later[-1], 'mp', down))  8.2 us
    ppermute x3, starting transfers between devices, shards(): later.append(lax.ppermute(later[-1], 'mp', down))  5.64 us
  transfers between devices with their start and end apart: 11, of which 6 were waited for; matrix products, arithmetic and copies ran while one was open for 27% of the time, Pallas kernels for 0%

profile of v1, /device:TPU:18, one launch (start us, length us, event | category | flops | bytes accessed | tf_op | source)
XLA Modules:
  0.0 255.5 jit_solution(14901001172727015877)
XLA Ops:
  7.2 0.7 all-gather.2.cloned.1.call-update
  8.0 2.0 copy.68
  10.0 1.1 fusion.4
  11.4 4.7 %fusion.6 = bf16[64,8192]{0,1:T(8,128)(2,1)S(1)} fusion(bf16[1,64,8192]{1,2,0:T(8,128)(2,1)} %copy-done, f32[8192]{0:T(1024)S(1)} %copy-done.4, f32[64]{0:T(128)S(1)} %add_rsqrt_fusion), kind=kLoop, calls=%fused_computation.9 | loop fusion | flops 2097152 | bytes 2130176 | tf_op jit(solution)/shard_map/convert_element_type | solution.py:73
  16.0 1.6 copy.69
  17.7 1.7 collective-permute-start.4
  19.4 12.7 %collective-permute-done = bf16[64,8192]{1,0:T(8,128)(2,1)S(1)} collective-permute-done((bf16[64,8192]{1,0:T(8,128)(2,1)}, bf16[64,8192]{1,0:T(8,128)(2,1)S(1)}, u32[]{:S(2)}, u32[]{:S(2)}) %collective-permute-start) | collective-permute-done | bytes 1048608 | tf_op jit(solution)/shard_map/ppermute | solution.py:79
  32.1 2.1 collective-permute-start.5
  34.3 12.2 %collective-permute-done.1 = bf16[64,8192]{1,0:T(8,128)(2,1)} collective-permute-done((bf16[64,8192]{1,0:T(8,128)(2,1)S(1)}, bf16[64,8192]{1,0:T(8,128)(2,1)}, u32[]{:S(2)}, u32[]{:S(2)}) %collective-permute-start.1) | collective-permute-done | bytes 1048608 | tf_op jit(solution)/shard_map/ppermute | solution.py:79
  47.9 1.8 collective-permute-start.6
  49.7 11.3 %collective-permute-done.2 = bf16[64,8192]{1,0:T(8,128)(2,1)} collective-permute-done((bf16[64,8192]{1,0:T(8,128)(2,1)}, bf16[64,8192]{1,0:T(8,128)(2,1)}, u32[]{:S(2)}, u32[]{:S(2)}) %collective-permute-start.2) | collective-permute-done | bytes 1048608 | tf_op jit(solution)/shard_map/ppermute | solution.py:79
  61.6 1.8 copy.74
  63.4 2.7 %copy.75 = bf16[64,8192]{0,1:T(8,128)(2,1)} copy(bf16[64,8192]{1,0:T(8,128)(2,1)} %collective-permute-done.4) | data formatting | bytes 2097152 | tf_op jit(solution)/shard_map/ppermute | solution.py:81
  66.2 2.7 %copy.73 = bf16[64,8192]{0,1:T(8,128)(2,1)} copy(bf16[64,8192]{1,0:T(8,128)(2,1)} %collective-permute-done.1) | data formatting | bytes 2097152 | tf_op jit(solution)/shard_map/ppermute | solution.py:79
  68.9 2.7 %copy.76 = bf16[64,8192]{0,1:T(8,128)(2,1)} copy(bf16[64,8192]{1,0:T(8,128)(2,1)} %collective-permute-done.5) | data formatting | bytes 2097152 | tf_op jit(solution)/shard_map/ppermute | solution.py:81
  71.6 2.7 %copy.72 = bf16[64,8192]{0,1:T(8,128)(2,1)} copy(bf16[64,8192]{1,0:T(8,128)(2,1)} %collective-permute-done.2) | data formatting | bytes 2097152 | tf_op jit(solution)/shard_map/ppermute | solution.py:79
  74.4 2.7 %copy.77 = bf16[64,8192]{0,1:T(8,128)(2,1)} copy(bf16[64,8192]{1,0:T(8,128)(2,1)} %collective-permute-done.6) | data formatting | bytes 2097152 | tf_op jit(solution)/shard_map/ppermute | solution.py:81
  77.1 2.8 %copy.71 = bf16[64,8192]{0,1:T(8,128)(2,1)} copy(bf16[64,8192]{1,0:T(8,128)(2,1)} %collective-permute-done.3) | data formatting | bytes 2097152 | tf_op jit(solution)/shard_map/ppermute | solution.py:79
  79.9 37.6 %concatenate.15 = bf16[1024,8192]{0,1:T(8,128)(2,1)} concatenate(bf16[64,8192]{0,1:T(8,128)(2,1)} %copy.71, bf16[64,8192]{0,1:T(8,128)(2,1)} %copy.72, bf16[64,8192]{0,1:T(8,128)(2,1)} %copy.73, bf16[64,8192]{0,1:T(8,128)(2,1)} %copy.74, bf16[64,8192]{0,1:T(8,128)(2,1)S(1)} %fusion.6, bf16[64,8192]{0,1:T(8,128)(2,1)} %copy.75, bf16[64,8192]{0,1:T(8,128)(2,1)} %copy.76, ...), dimensions={0} | concatenate | bytes 33554432 | tf_op jit(solution)/shard_map/jit(_roll_dynamic)/concatenate | solution.py:83
  117.5 9.5 %fusion.10 = bf16[512,256]{0,1:T(8,128)(2,1)S(1)} fusion(bf16[1024,8,2,128]{3,2,1,0:T(2,128)(2,1)} %bitcast.128, bf16[1024,8192]{0,1:T(8,128)(2,1)} %concatenate.15, s32[]{:T(128)S(6)} %select_n.21), kind=kOutput, calls=%fused_computation.15 | convolution fusion | flops 2147614720 | bytes 12845060 | tf_op jit(solution)/shard_map/dot_general | solution.py:87
  127.6 0.3 convolution_bitcast_fusion.1
  127.9 0.3 multiply_reduce_fusion
  128.7 11.1 %convolution_convert_fusion = bf16[8192,2,128]{2,0,1:T(8,128)(2,1)} fusion(bf16[1024,8192]{0,1:T(8,128)(2,1)} %concatenate.15, s32[]{:T(128)S(6)} %select_n.21, f32[640,1,1,128]{0,3,2,1:T(8,128)S(1)} %convolution_bitcast_fusion.1, f32[640,1,1,128]{0,3,2,1:T(8,128)S(1)} %fusion.17), kind=kOutput, calls=%fused_computation | convolution fusion | flops 2150105088 | bytes 13238276 | tf_op jit(solution)/shard_map/dot_general | solution.py:123
  139.9 66.9 %reduce-scatter.3.cloned.1.call-done = bf16[1024,2,128]{2,0,1:T(8,128)(2,1)} async-done(((bf16[8192,2,128]{2,0,1:T(8,128)(2,1)}), bf16[1024,2,128]{2,0,1:T(8,128)(2,1)}) %reduce-scatter.3.cloned.1.call-update) | async-done | bytes 524304 | tf_op jit(solution)/shard_map/reduce_scatter | solution.py:20
  207.0 30.8 %reduce-scatter.5.cloned.1.call-done = bf16[256,2,128]{2,0,1:T(8,128)(2,1)} async-done(((bf16[1024,2,128]{2,0,1:T(8,128)(2,1)}), bf16[256,2,128]{2,0,1:T(8,128)(2,1)}) %reduce-scatter.5.cloned.1.call-update) | async-done | bytes 131088 | tf_op jit(solution)/shard_map/reduce_scatter | solution.py:20
  237.8 1.6 broadcast_in_dim.24
  239.4 3.4 %all-to-all-start = ((bf16[2,256,2,128]{3,1,2,0:T(8,128)(2,1)}), bf16[2,256,2,128]{3,1,2,0:T(8,128)(2,1)S(1)}, u32[]{:S(2)}, u32[]{:S(2)}) async-start(bf16[2,256,2,128]{3,1,2,0:T(8,128)(2,1)} %broadcast_in_dim.24), calls=%async_computation.2 | async-start | bytes 524288 | tf_op jit(solution)/shard_map/all_to_all | solution.py:26
  242.9 0.8 copy.101
  243.7 0.8 copy.100
  244.7 0.7 copy.99
  245.5 2.6 %all-to-all-done = bf16[2,256,2,128]{3,1,2,0:T(8,128)(2,1)S(1)} async-done(((bf16[2,256,2,128]{3,1,2,0:T(8,128)(2,1)}), bf16[2,256,2,128]{3,1,2,0:T(8,128)(2,1)S(1)}, u32[]{:S(2)}, u32[]{:S(2)}) %all-to-all-start) | async-done | bytes 262176 | tf_op jit(solution)/shard_map/all_to_all | solution.py:26
  248.1 0.9 copy.102
  (50 shorter events, 2.7 us)
Async XLA Ops:
  7.2 4.2 %copy-start.4 = (f32[8192]{0:T(1024)S(1)}, f32[8192]{0:T(1024)}, u32[]{:S(2)}) copy-start(f32[8192]{0:T(1024)} %param.11) | copy-start | bytes 98308
  7.2 110.3 %all-gather.2.cloned.1.call-start = ((), (), s32[]{:S(2)}) async-start(), calls=%async_computation.3 | async-start | bytes 4325376 | tf_op jit(solution)/shard_map/all_gather | solution.py:85
  7.9 198.8 %reduce-scatter.3.cloned.1.call-start = ((), (), s32[]{:S(2)}) async-start(), calls=%async_computation.4 | async-start | bytes 4718592 | tf_op jit(solution)/shard_map/reduce_scatter | solution.py:20
  10.0 1.3 copy-start
  11.3 35.8 %copy-start.1 = (bf16[1,128,2,128]{3,2,1,0:T(2,128)(2,1)S(1)}, bf16[1,128,2,128]{3,2,1,0:T(2,128)(2,1)}, u32[]{:S(2)}) copy-start(bf16[1,128,2,128]{3,2,1,0:T(2,128)(2,1)} %param.14) | copy-start | bytes 196612
  11.3 35.8 %copy-start.2 = (bf16[1,128,256]{2,1,0:T(8,128)(2,1)S(1)}, bf16[1,128,256]{2,1,0:T(8,128)(2,1)}, u32[]{:S(2)}) copy-start(bf16[1,128,256]{2,1,0:T(8,128)(2,1)} %param.13) | copy-start | bytes 196612
  11.3 49.7 %copy-start.3 = (bf16[1,128,256]{2,1,0:T(8,128)(2,1)S(1)}, bf16[1,128,256]{2,1,0:T(8,128)(2,1)}, u32[]{:S(2)}) copy-start(bf16[1,128,256]{2,1,0:T(8,128)(2,1)} %param.15) | copy-start | bytes 196612
  11.3 49.9 %copy-start.5 = (s32[1,128]{1,0:T(1,128)S(1)}, s32[1,128]{1,0:T(1,128)}, u32[]{:S(2)}) copy-start(s32[1,128]{1,0:T(1,128)} %param.17) | copy-start | bytes 1540
  11.4 50.0 %copy-start.6 = (s32[1,512]{1,0:T(1,128)S(1)}, s32[1,512]{1,0:T(1,128)}, u32[]{:S(2)}) copy-start(s32[1,512]{1,0:T(1,128)} %param.16) | copy-start | bytes 6148
  17.7 14.4 %collective-permute-start = (bf16[64,8192]{1,0:T(8,128)(2,1)}, bf16[64,8192]{1,0:T(8,128)(2,1)S(1)}, u32[]{:S(2)}, u32[]{:S(2)}) collective-permute-start(bf16[64,8192]{1,0:T(8,128)(2,1)} %copy.69), channel_id=1, source_target_pairs={{0,1},{1,2},{2,3},{3,4},{4,5},{5,6},{6,7},{7,0},{8,9},{9,10},{10,1... | collective-permute-start | bytes 3145736 | tf_op jit(solution)/shard_map/ppermute | solution.py:79
  17.7 14.4 %collective-permute-start.4 = (bf16[64,8192]{1,0:T(8,128)(2,1)}, bf16[64,8192]{1,0:T(8,128)(2,1)}, u32[]{:S(2)}, u32[]{:S(2)}) collective-permute-start(bf16[64,8192]{1,0:T(8,128)(2,1)} %copy.69), channel_id=1, source_target_pairs={{0,7},{1,0},{2,1},{3,2},{4,3},{5,4},{6,5},{7,6},{8,15},{9,8},{10,9... | collective-permute-start | bytes 3145736 | tf_op jit(solution)/shard_map/ppermute | solution.py:81
  32.1 14.3 %collective-permute-start.1 = (bf16[64,8192]{1,0:T(8,128)(2,1)S(1)}, bf16[64,8192]{1,0:T(8,128)(2,1)}, u32[]{:S(2)}, u32[]{:S(2)}) collective-permute-start(bf16[64,8192]{1,0:T(8,128)(2,1)S(1)} %collective-permute-done), channel_id=1, source_target_pairs={{0,1},{1,2},{2,3},{3,4},{4,5},{5,6},{6,7},{7,0},{8,9},{9,10},{10,1... | collective-permute-start | bytes 3145736 | tf_op jit(solution)/shard_map/ppermute | solution.py:79
  32.1 15.8 %collective-permute-start.5 = (bf16[64,8192]{1,0:T(8,128)(2,1)}, bf16[64,8192]{1,0:T(8,128)(2,1)}, u32[]{:S(2)}, u32[]{:S(2)}) collective-permute-start(bf16[64,8192]{1,0:T(8,128)(2,1)} %collective-permute-done.4), channel_id=1, source_target_pairs={{0,7},{1,0},{2,1},{3,2},{4,3},{5,4},{6,5},{7,6},{8,15},{9,8},{10,9... | collective-permute-start | bytes 3145736 | tf_op jit(solution)/shard_map/ppermute | solution.py:81
  46.5 14.5 %collective-permute-start.2 = (bf16[64,8192]{1,0:T(8,128)(2,1)}, bf16[64,8192]{1,0:T(8,128)(2,1)}, u32[]{:S(2)}, u32[]{:S(2)}) collective-permute-start(bf16[64,8192]{1,0:T(8,128)(2,1)} %collective-permute-done.1), channel_id=1, source_target_pairs={{0,1},{1,2},{2,3},{3,4},{4,5},{5,6},{6,7},{7,0},{8,9},{9,10},{10,1... | collective-permute-start | bytes 3145736 | tf_op jit(solution)/shard_map/ppermute | solution.py:79
  47.9 26.4 %collective-permute-start.6 = (bf16[64,8192]{1,0:T(8,128)(2,1)}, bf16[64,8192]{1,0:T(8,128)(2,1)}, u32[]{:S(2)}, u32[]{:S(2)}) collective-permute-start(bf16[64,8192]{1,0:T(8,128)(2,1)} %collective-permute-done.5), channel_id=1, source_target_pairs={{0,7},{1,0},{2,1},{3,2},{4,3},{5,4},{6,5},{7,6},{8,15},{9,8},{10,9... | collective-permute-start | bytes 3145736 | tf_op jit(solution)/shard_map/ppermute | solution.py:81
  61.0 16.1 %collective-permute-start.3 = (bf16[64,8192]{1,0:T(8,128)(2,1)}, bf16[64,8192]{1,0:T(8,128)(2,1)}, u32[]{:S(2)}, u32[]{:S(2)}) collective-permute-start(bf16[64,8192]{1,0:T(8,128)(2,1)} %collective-permute-done.2), channel_id=1, source_target_pairs={{0,1},{1,2},{2,3},{3,4},{4,5},{5,6},{6,7},{7,0},{8,9},{9,10},{10,1... | collective-permute-start | bytes 3145736 | tf_op jit(solution)/shard_map/ppermute | solution.py:79
  139.8 98.0 %reduce-scatter.5.cloned.1.call-start = ((), (), s32[]{:S(2)}) async-start(), calls=%async_computation.5 | async-start | bytes 655360 | tf_op jit(solution)/shard_map/reduce_scatter | solution.py:20
  239.4 8.6 %all-to-all-start = ((bf16[2,256,2,128]{3,1,2,0:T(8,128)(2,1)}), bf16[2,256,2,128]{3,1,2,0:T(8,128)(2,1)S(1)}, u32[]{:S(2)}, u32[]{:S(2)}) async-start(bf16[2,256,2,128]{3,1,2,0:T(8,128)(2,1)} %broadcast_in_dim.24), calls=%async_computation.2 | async-start | bytes 524288 | tf_op jit(solution)/shard_map/all_to_all | solution.py:26
Sparse Core Ops, SparseCore 0:
  11.2 105.5 all-gather.1
  139.9 66.7 reduce-scatter.2
  209.6 28.1 reduce-scatter.4
